TPU v7x, 32 devices: a whole 2x2x4 slice. The times are simulated.
32 devices in a mesh: groups: 2 (over y), tensor: 4 (over z), frames: 4 (over x, core).
Axes of the slice: x: 2, y: 2, z: 4, core: 2. Of those that a mesh axis runs over, the one named last changes fastest.
Arguments:
- patches: bfloat16 [256, 16, 3072], P('tensor', ('groups', 'frames')), parts along dimension 1, may hold values from -12 to 12
- ln_gain: float32 [3072], replicated, may hold values from 0.5 to 1.5
- in_weight: bfloat16 [3072, 4, 768], P('frames', 'tensor'), may hold values from -0.109375 to 0.109375
- q_gain: float32 [4, 128], P('tensor'), may hold values from 0.1 to 1.9
- k_gain: float32 [4, 128], P('tensor'), may hold values from 0.1 to 1.9
- out_weight: bfloat16 [4, 512, 3072], P('tensor', None, 'frames'), may hold values from -0.25 to 0.25
Outputs:
- encoded: bfloat16 [256, 16, 3072], P('tensor', ('groups', 'frames')), parts along dimension 1
There are 2 independent parts, one for each index of `groups`. A program takes and returns all parts, laid end to end along the dimension named above; an argument that names none is the same for every part. Nothing has to cross between parts.
All inputs are finite; a program needn't handle non-finite values.
Results may differ from a plain program's by a relative error of at most 0.022.
Values may be sent and summed in bfloat16 or wider, within the bound.
A program may use at most 64 MiB of HBM per device.

v0:
```python
import math

import jax
import jax.numpy as jnp
from jax import lax
from jax.sharding import PartitionSpec as P


def layer_norm(values, gain_vec):
    mean_val = jnp.mean(values, axis=-1, keepdims=True)
    centered = values - mean_val
    variance = jnp.mean(centered * centered, axis=-1, keepdims=True)
    return centered * lax.rsqrt(variance + 1e-06) * gain_vec


def local(patches, ln_gain, in_weight, q_gain, k_gain, out_weight):
    head_dim = q_gain.shape[1]
    normed = layer_norm(patches.astype(jnp.float32), ln_gain).astype(jnp.bfloat16)
    in_local = in_weight[:, 0, :]
    out_local = out_weight[0]
    every_patch = lax.all_gather(normed, "tensor", axis=0, tiled=True)
    joined_cols = jnp.einsum(
        "qye,ea->qya",
        every_patch,
        lax.all_gather(in_local, "frames", axis=0, tiled=True),
        preferred_element_type=jnp.float32,
    )
    query_slice = layer_norm(joined_cols[..., :head_dim], q_gain[0])
    key_slice = layer_norm(joined_cols[..., head_dim : 2 * head_dim], k_gain[0])
    value_slice = joined_cols[..., 2 * head_dim : 3 * head_dim]
    hidden = jax.nn.gelu(joined_cols[..., 3 * head_dim :], approximate=False)
    prepared = jnp.concatenate([query_slice, key_slice, value_slice, hidden], axis=-1).astype(
        jnp.bfloat16
    )
    query_slice = prepared[..., :head_dim]
    key_slice = prepared[..., head_dim : 2 * head_dim]
    value_slice = prepared[..., 2 * head_dim : 3 * head_dim]
    attention_logits = jnp.einsum(
        "ldg,bdg->dlb", query_slice, key_slice, preferred_element_type=jnp.float32
    ) * (1.0 / math.sqrt(head_dim))
    exponent_scores = jnp.exp(attention_logits)
    softmax_total = jnp.sum(exponent_scores, axis=-1)
    attention_output = jnp.einsum(
        "jdl,ljg->djg",
        exponent_scores.astype(jnp.bfloat16),
        value_slice,
        preferred_element_type=jnp.float32,
    )
    attention_output = attention_output / jnp.transpose(softmax_total)[:, :, None]
    blended_rows = jnp.concatenate(
        [attention_output.astype(jnp.bfloat16), prepared[..., 3 * head_dim :]], axis=-1
    )
    combined_output = lax.all_gather(out_local, "frames", axis=1, tiled=True)
    summed = lax.psum_scatter(
        jnp.einsum(
            "vto,ox->vtx", blended_rows, combined_output, preferred_element_type=jnp.float32
        ).astype(jnp.bfloat16),
        "tensor",
        scatter_dimension=0,
        tiled=True,
    ).astype(jnp.float32)
    return (patches.astype(jnp.float32) + summed).astype(jnp.bfloat16)


def solution(mesh):
    return jax.shard_map(
        local,
        mesh=mesh,
        in_specs=(
            P("tensor", ("groups", "frames"), None),
            P(),
            P("frames", "tensor", None),
            P("tensor", None),
            P("tensor", None),
            P("tensor", None, "frames"),
        ),
        out_specs=P("tensor", ("groups", "frames"), None),
        check_vma=False,
    )
```

profile of v0, /device:TPU:0, one launch (start us, length us, event | category | flops | bytes accessed | tf_op | source)
XLA Modules:
  0.0 220.3 jit_solution(9089769881547310153)
XLA Ops:
  6.5 1.4 convert_reduce_fusion
  7.9 1.5 fusion.5
  9.5 1.2 fusion.7
  10.7 0.0 all-gather.6.cloned.1.call-update
  10.7 0.0 all-gather.8.cloned.1.call-start
  10.8 0.7 all-gather.8.cloned.1.call-update
  11.5 0.0 all-gather.10.cloned.1.call-start
  11.5 0.7 all-gather.10.cloned.1.call-update
  12.2 0.0 copy-start.2
  12.2 0.0 reduce-scatter.2.cloned.1.call-start
  12.3 64.8 %all-gather.6.cloned.1.call-done = bf16[256,2,3072]{2,0,1:T(8,128)(2,1)} async-done(((bf16[64,2,3072]{2,0,1:T(8,128)(2,1)}), bf16[256,2,3072]{2,0,1:T(8,128)(2,1)}) %all-gather.6.cloned.1.call-update) | async-done | bytes 3145744 | tf_op jit(solution)/shard_map/all_gather | solution.py:21
  77.0 37.7 %all-gather.8.cloned.1.call-done = bf16[3072,1,768]{2,0,1:T(8,128)(2,1)} async-done(((bf16[768,1,768]{2,0,1:T(8,128)(2,1)}), bf16[3072,1,768]{2,0,1:T(8,128)(2,1)}) %all-gather.8.cloned.1.call-update) | async-done | bytes 4718608 | tf_op jit(solution)/shard_map/all_gather | solution.py:25
  114.8 5.9 %fusion = f32[256,2,768]{2,0,1:T(8,128)S(1)} fusion(bf16[256,2,3072]{2,0,1:T(8,128)(2,1)} %all-gather.6.cloned.1.call-done, bf16[3072,1,768]{2,0,1:T(8,128)(2,1)} %all-gather.8.cloned.1.call-done), kind=kOutput, calls=%fused_computation | convolution fusion | flops 2415919104 | bytes 9437184 | tf_op jit(solution)/shard_map/qye,ea->qya/dot_general | solution.py:22
  120.7 0.2 slice_reduce_fusion.1
  120.9 0.4 multiply_reduce_fusion.1
  121.3 0.5 fusion.33
  121.8 0.3 fusion.11
  122.1 1.7 fusion.14
  123.8 21.1 %all-gather.10.cloned.1.call-done = bf16[1,512,3072]{2,1,0:T(8,128)(2,1)} async-done(((bf16[1,512,768]{2,1,0:T(8,128)(2,1)}), bf16[1,512,3072]{2,1,0:T(8,128)(2,1)}) %all-gather.10.cloned.1.call-update) | async-done | bytes 3145744 | tf_op jit(solution)/shard_map/all_gather | solution.py:53
  144.9 5.4 %convolution_convert_fusion = bf16[256,2,3072]{2,0,1:T(8,128)(2,1)} fusion(bf16[1,512,3072]{2,1,0:T(8,128)(2,1)} %all-gather.10.cloned.1.call-done, bf16[256,2,384]{2,0,1:T(8,128)(2,1)S(1)} %fusion.14, bf16[256,2,128]{2,0,1:T(8,128)(2,1)S(1)} %fusion.11), kind=kOutput, calls=%fused_computation.2 | convolution fusion | flops 1613234176 | bytes 6815744 | tf_op jit(solution)/shard_map/vto,ox->vtx/dot_general | solution.py:55
  150.3 0.0 reduce-scatter.2.cloned.1.call-update
  150.3 60.4 %reduce-scatter.2.cloned.1.call-done = bf16[64,2,3072]{2,0,1:T(8,128)(2,1)} async-done(((bf16[256,2,3072]{2,0,1:T(8,128)(2,1)}), bf16[64,2,3072]{2,0,1:T(8,128)(2,1)}) %reduce-scatter.2.cloned.1.call-update) | async-done | bytes 786448 | tf_op jit(solution)/shard_map/reduce_scatter | solution.py:54
  210.7 1.3 fusion.8
  212.1 1.7 copy.8
  (13 shorter events, 0.1 us)
Async XLA Ops:
  6.5 2.9 %copy-start = (bf16[64,2,3072]{2,1,0:T(2,128)(2,1)S(1)}, bf16[64,2,3072]{2,1,0:T(2,128)(2,1)}, u32[]{:S(2)}) copy-start(bf16[64,2,3072]{2,1,0:T(2,128)(2,1)} %param.6) | copy-start | bytes 2359300
  6.5 2.9 %copy-start.1 = (f32[3072]{0:T(1024)S(1)}, f32[3072]{0:T(1024)}, u32[]{:S(2)}) copy-start(f32[3072]{0:T(1024)} %param.7) | copy-start | bytes 36868
  6.5 70.5 %all-gather.6.cloned.1.call-start = ((), (), s32[]{:S(2)}) async-start(), calls=%async_computation.1 | async-start | bytes 3932160 | tf_op jit(solution)/shard_map/all_gather | solution.py:21
  10.7 104.1 %all-gather.8.cloned.1.call-start = ((), (), s32[]{:S(2)}) async-start(), calls=%async_computation.3 | async-start | bytes 5898240 | tf_op jit(solution)/shard_map/all_gather | solution.py:25
  11.5 133.5 %all-gather.10.cloned.1.call-start = ((), (), s32[]{:S(2)}) async-start(), calls=%async_computation.4 | async-start | bytes 3932160 | tf_op jit(solution)/shard_map/all_gather | solution.py:53
  12.2 109.1 %copy-start.2 = (f32[1,128]{1,0:T(1,128)S(1)}, f32[1,128]{1,0:T(1,128)}, u32[]{:S(2)}) copy-start(f32[1,128]{1,0:T(1,128)} %param.10) | copy-start | bytes 1540
  12.2 109.1 %copy-start.3 = (f32[1,128]{1,0:T(1,128)S(1)}, f32[1,128]{1,0:T(1,128)}, u32[]{:S(2)}) copy-start(f32[1,128]{1,0:T(1,128)} %param.9) | copy-start | bytes 1540
  12.2 198.5 %reduce-scatter.2.cloned.1.call-start = ((), (), s32[]{:S(2)}) async-start(), calls=%async_computation.2 | async-start | bytes 3932160 | tf_op jit(solution)/shard_map/reduce_scatter | solution.py:54
Sparse Core Ops, SparseCore 0:
  10.8 66.1 all-gather.5
  78.6 36.1 all-gather.7
  116.3 28.5 all-gather.9
  150.4 60.2 reduce-scatter.1
where the time goes:
time: 221 us; the launch traced here: 220 us
  waiting for transfers between devices  185 us (84%)
  between operations  13.2 us (6%)
  matrix products  12 us (5%)
  other arithmetic  7.81 us (4%)
    all_gather x1, waiting for transfers between devices, local(): every_patch = lax.all_gather(normed, 'tensor', axis=0, tiled=True)  64.8 us
    reduce_scatter x1, waiting for transfers between devices, local(): lax.psum_scatter(jnp.einsum('vto,ox->vtx', blended_rows, combined_output,...  60.4 us
    all_gather x1, waiting for transfers between devices, local(): lax.all_gather(in_local, 'frames', axis=0, tiled=True)  37.7 us
    all_gather x1, waiting for transfers between devices, local(): combined_output = lax.all_gather(out_local, 'frames', axis=1, tiled=True)  21.1 us
    dot_general x1, matrix products, local(): jnp.einsum('qye,ea->qya', every_patch, lax.all_gather(in_local, 'frames',...  5.89 us
    dot_general x1, matrix products, local(): jnp.einsum('vto,ox->vtx', blended_rows, combined_output, preferred_elemen...  5.36 us
  transfers between devices with their start and end apart: 4, of which 4 were waited for; matrix products, arithmetic and copies ran while one was open for 4% of the time, Pallas kernels for 0%

commit v1 on v0

v1 whole, which is shorter than its diff:
```python
import functools
import math

import jax
import jax.numpy as jnp
from jax import lax
from jax.experimental import pallas as pl
from jax.experimental.pallas import tpu as pltpu
from jax.sharding import PartitionSpec as P

MESH = pl.DeviceIdType.MESH


def norm(values, gain_vec):
    mean_val = jnp.mean(values, axis=-1, keepdims=True)
    centered = values - mean_val
    variance = jnp.mean(centered * centered, axis=-1, keepdims=True)
    return centered * lax.rsqrt(variance + 1e-06) * gain_vec


def kernel(ng, nt, nf, nlo, subs, x_ref, gain_ref, win_ref, qg_ref, kg_ref, wout_ref, out_ref,
           xg, w_in, w_out, joined, blended, part, rbuf,
           ag_send, ag_recv, rs_send, rs_recv, ws_send, ws_recv, own_sem):
    g, t, f = lax.axis_index("groups"), lax.axis_index("tensor"), lax.axis_index("frames")
    frames, rows, width = x_ref.shape
    head_dim = qg_ref.shape[1]
    nhi = nf // nlo
    hi, lo = f // nlo, f % nlo
    sibling = {"frames": hi * nlo + (nlo - 1 - lo)}
    right, left = {"tensor": lax.rem(t + 1, nt)}, {"tensor": lax.rem(t + nt - 1, nt)}

    barrier = pltpu.get_barrier_semaphore()

    def greet(device):
        pl.semaphore_signal(barrier, inc=1, device_id=device, device_id_type=MESH)

    pl.when(t + 1 < nt)(lambda: greet(right))
    pl.when(t > 0)(lambda: greet(left))
    if nlo > 1:
        greet(sibling)
    for j in range(1, nhi):
        greet({"frames": lax.rem(hi + j, nhi) * nlo + lo})
    for k in range(1, ng):
        greet({"groups": lax.rem(g + k, ng)})
    fixed = (nlo - 1) + (nhi - 1) + (ng - 1)
    pl.semaphore_wait(barrier, fixed + jnp.where(t + 1 < nt, 1, 0) + jnp.where(t > 0, 1, 0))

    held, given = (w_in, w_out), (win_ref, wout_ref)

    def piece(w, shard, section, sub):
        size = held[w].shape[1] // (ng * subs)
        start = pl.multiple_of((section * subs + sub) * size, size)
        return held[w].at[shard, pl.ds(start, size), :]

    def own_piece(w, section, sub):
        size = held[w].shape[1] // (ng * subs)
        start = pl.multiple_of((section * subs + sub) * size, size)
        return given[w].at[pl.ds(start, size), :]

    def move(w, shard, section, sub, slot, device, own=False):
        return pltpu.make_async_remote_copy(
            src_ref=own_piece(w, section, sub) if own else piece(w, shard, section, sub),
            dst_ref=piece(w, shard, section, sub),
            send_sem=ws_send.at[w, shard, section, sub, slot],
            recv_sem=ws_recv.at[w, shard, section, sub],
            device_id=device,
            device_id_type=MESH,
        )

    def w_own_across(w, act):
        for sub in range(subs):
            for j in range(1, nhi):
                act(move(w, f, g, sub, j - 1, {"frames": lax.rem(hi + j, nhi) * nlo + lo}, True))

    last = max(nhi - 1, ng - 1)

    def w_own_sibling(w, act):
        if nlo > 1:
            for section in range(ng):
                for sub in range(subs):
                    act(move(w, f, section, sub, last, sibling, True))

    def w_relay(w, sub, act, wait):
        for j in range(1, nhi):
            shard = lax.rem(hi + nhi - j, nhi) * nlo + lo
            if wait:
                move(w, shard, g, sub, 0, sibling).wait_recv()
            for k in range(1, ng):
                act(move(w, shard, g, sub, k - 1, {"groups": lax.rem(g + k, ng)}))
            if nlo > 1:
                act(move(w, shard, g, sub, last, sibling))

    def w_relay_two(w, sub, act, wait):
        for j in range(1, nhi):
            shard = lax.rem(hi + nhi - j, nhi) * nlo + lo
            for k in range(1, ng):
                section = lax.rem(g + k, ng)
                if wait:
                    move(w, shard, section, sub, 0, sibling).wait_recv()
                if nlo > 1:
                    act(move(w, shard, section, sub, last, sibling))

    def w_finish(w):
        if nlo > 1:
            for j in range(nhi):
                shard = j * nlo + (nlo - 1 - lo)
                for section in range(ng):
                    for sub in range(subs):
                        move(w, shard, section, sub, 0, sibling).wait_recv()
        pltpu.make_async_copy(given[w], held[w].at[f], own_sem.at[w]).wait()

    def start(copy):
        copy.start()

    def sent(copy):
        copy.wait_send()

    def w_sent(w):
        w_own_across(w, sent)
        w_own_sibling(w, sent)
        for sub in range(subs):
            w_relay(w, sub, sent, False)
            w_relay_two(w, sub, sent, False)

    def block(ref, fr, b):
        return ref.at[fr, pl.ds(pl.multiple_of(b * rows, rows), rows), :]

    def ag_copy(fr, b, way):
        return pltpu.make_async_remote_copy(
            src_ref=block(xg, fr, b),
            dst_ref=block(xg, fr, b),
            send_sem=ag_send.at[fr, way, b],
            recv_sem=ag_recv.at[fr, b],
            device_id=right if way == 0 else left,
            device_id_type=MESH,
        )

    def ag_own(fr, act):
        pl.when(t + 1 < nt)(lambda: act(ag_copy(fr, t, 0)))
        pl.when(t > 0)(lambda: act(ag_copy(fr, t, 1)))

    def ag_step(fr, s, act, wait):
        b = t - 1 - s

        @pl.when(b >= 0)
        def _():
            if wait:
                ag_copy(fr, b, 0).wait_recv()
            pl.when(t + 1 < nt)(lambda: act(ag_copy(fr, b, 0)))

        c = t + 1 + s

        @pl.when(c < nt)
        def _():
            if wait:
                ag_copy(fr, c, 1).wait_recv()
            pl.when(t > 0)(lambda: act(ag_copy(fr, c, 1)))

    def rs_copy(fr, d, way, first):
        slot = d if way == 0 else jnp.where(d == t - 1, nt, d)
        return pltpu.make_async_remote_copy(
            src_ref=block(part, fr, d) if first else rbuf.at[fr, d],
            dst_ref=rbuf.at[fr, slot],
            send_sem=rs_send.at[fr, d],
            recv_sem=rs_recv.at[fr, slot],
            device_id=right if way == 0 else left,
            device_id_type=MESH,
        )

    def rs_arrived(fr, slot):
        pltpu.make_async_remote_copy(
            src_ref=rbuf.at[fr, slot],
            dst_ref=rbuf.at[fr, slot],
            send_sem=rs_send.at[fr, 0],
            recv_sem=rs_recv.at[fr, slot],
            device_id=right,
            device_id_type=MESH,
        ).wait_recv()

    def rs_send_on(fr, d, way, edge):
        @pl.when(edge)
        def _():
            rs_copy(fr, d, way, True).start()

        @pl.when(jnp.logical_not(edge))
        def _():
            rs_arrived(fr, d)
            mine = block(part, fr, d)[...].astype(jnp.float32)
            rbuf[fr, d] = (rbuf[fr, d].astype(jnp.float32) + mine).astype(jnp.bfloat16)
            rs_copy(fr, d, way, False).start()

    def rs_step(fr, s):
        d = nt - 1 - s
        pl.when(d > t)(lambda: rs_send_on(fr, d, 0, t == 0))
        pl.when(s < t)(lambda: rs_send_on(fr, s, 1, t == nt - 1))

    def rs_sent(fr):
        for d in range(nt):
            @pl.when(d != t)
            def _():
                rs_copy(fr, d, 0, True).wait_send()

    def rs_finish(fr):
        out_ref[fr] = (x_ref[fr].astype(jnp.float32) + block(part, fr, t)[...].astype(jnp.float32)).astype(jnp.float32)

        @pl.when(t > 0)
        def _():
            rs_arrived(fr, t)
            out_ref[fr] += rbuf[fr, t].astype(jnp.float32)

        @pl.when(t + 1 < nt)
        def _():
            rs_arrived(fr, nt)
            out_ref[fr] += rbuf[fr, nt].astype(jnp.float32)

    def normalise(fr):
        values = norm(x_ref[fr].astype(jnp.float32), gain_ref[...]).astype(jnp.bfloat16)
        block(xg, fr, t)[...] = values

    def project(fr):
        tile = 256 if joined.shape[1] % 256 == 0 else joined.shape[1]

        @pl.loop(0, joined.shape[1] // tile)
        def _(n):
            cols = pl.ds(pl.multiple_of(n * tile, tile), tile)
            weight = w_in[:, :, cols].reshape(width, tile)
            joined[:, cols] = jnp.dot(xg[fr], weight, preferred_element_type=jnp.float32)

        query = norm(joined[:, :head_dim], qg_ref[...]).astype(jnp.bfloat16)
        key = norm(joined[:, head_dim:2 * head_dim], kg_ref[...]).astype(jnp.bfloat16)
        value = joined[:, 2 * head_dim:3 * head_dim].astype(jnp.bfloat16)
        raw = joined[:, 3 * head_dim:]
        blended[:, head_dim:] = (0.5 * raw * (1.0 + lax.erf(raw * math.sqrt(0.5)))).astype(jnp.bfloat16)
        scores = lax.dot_general(query, key, (((1,), (1,)), ((), ())), preferred_element_type=jnp.float32)
        exp_scores = jnp.exp(scores * (1.0 / math.sqrt(head_dim)))
        total = jnp.sum(exp_scores, axis=-1, keepdims=True)
        attended = jnp.dot(exp_scores.astype(jnp.bfloat16), value, preferred_element_type=jnp.float32)
        blended[:, :head_dim] = (attended / total).astype(jnp.bfloat16)

    def contribute(fr):
        cols = w_out.shape[2]

        @pl.loop(0, nf)
        def _(n):
            part[fr, :, pl.ds(pl.multiple_of(n * cols, cols), cols)] = jnp.dot(
                blended[...], w_out[n], preferred_element_type=jnp.float32
            ).astype(jnp.bfloat16)

    for w in range(2):
        pltpu.make_async_copy(given[w], held[w].at[f], own_sem.at[w]).start()
    w_own_across(0, start)
    w_own_sibling(0, start)
    normalise(0)
    ag_own(0, start)
    for fr in range(1, frames):
        normalise(fr)

    tasks = [functools.partial(w_relay, 0, sub, start, True) for sub in range(subs)]
    tasks += [functools.partial(w_own_across, 1, start), functools.partial(w_own_sibling, 1, start)]
    tasks += [functools.partial(w_relay_two, 0, sub, start, True) for sub in range(subs)]
    tasks += [functools.partial(w_relay, 1, sub, start, True) for sub in range(subs)]
    done = 0
    for s in range(nt - 1):
        until = -(-len(tasks) * (s + 1) // (nt - 1))
        for task in tasks[done:until]:
            task()
        done = until
        ag_step(0, s, start, True)
    for fr in range(frames):
        if fr + 1 < frames:
            ag_own(fr + 1, start)
        if fr == 0:
            w_finish(0)
        project(fr)
        if fr == 0:
            for sub in range(subs):
                w_relay_two(1, sub, start, True)
            w_finish(1)
        contribute(fr)
        for s in range(nt - 1):
            if fr + 1 < frames:
                ag_step(fr + 1, s, start, True)
            rs_step(fr, s)
    for fr in range(frames):
        rs_finish(fr)

    for w in range(2):
        w_sent(w)
    for fr in range(frames):
        ag_own(fr, sent)
        for s in range(nt - 1):
            ag_step(fr, s, sent, False)
        rs_sent(fr)


def local(ng, nt, nf, patches, ln_gain, in_weight, q_gain, k_gain, out_weight):
    rows, frames, width = patches.shape
    depth, _, joined_cols = in_weight.shape
    _, out_rows, out_cols = out_weight.shape
    nlo = 2 if nf % 2 == 0 else 1
    nhi = nf // nlo
    subs = 2 if depth % (ng * 32) == 0 and out_rows % (ng * 32) == 0 else 1
    slots = max(nhi - 1, ng - 1) + 1
    everyone = nt * rows
    vmem = pl.BlockSpec(memory_space=pltpu.VMEM)
    hbm = pl.BlockSpec(memory_space=pl.ANY)
    bf16, f32 = jnp.bfloat16, jnp.float32
    dma = pltpu.SemaphoreType.DMA
    summed = pl.pallas_call(
        functools.partial(kernel, ng, nt, nf, nlo, subs),
        out_shape=jax.ShapeDtypeStruct((frames, rows, width), f32),
        in_specs=[vmem, vmem, hbm, vmem, vmem, hbm],
        out_specs=vmem,
        scratch_shapes=[
            pltpu.VMEM((frames, everyone, width), bf16),
            pltpu.VMEM((nf, depth, joined_cols), bf16),
            pltpu.VMEM((nf, out_rows, out_cols), bf16),
            pltpu.VMEM((everyone, joined_cols), f32),
            pltpu.VMEM((everyone, out_rows), bf16),
            pltpu.VMEM((frames, everyone, width), bf16),
            pltpu.VMEM((frames, nt + 1, rows, width), bf16),
            dma((frames, 2, nt)),
            dma((frames, nt)),
            dma((frames, nt)),
            dma((frames, nt + 1)),
            dma((2, nf, ng, subs, slots)),
            dma((2, nf, ng, subs)),
            dma((2,)),
        ],
        compiler_params=pltpu.CompilerParams(
            collective_id=0, has_side_effects=True, vmem_limit_bytes=48 * 1024 * 1024
        ),
    )(
        jnp.transpose(patches, (1, 0, 2)),
        ln_gain.reshape(1, width),
        in_weight.reshape(depth, joined_cols),
        q_gain,
        k_gain,
        out_weight.reshape(out_rows, out_cols),
    )
    return jnp.transpose(summed, (1, 0, 2)).astype(jnp.bfloat16)


def solution(mesh):
    sizes = [mesh.shape[name] for name in ("groups", "tensor", "frames")]
    return jax.shard_map(
        functools.partial(local, *sizes),
        mesh=mesh,
        in_specs=(
            P("tensor", ("groups", "frames"), None),
            P(),
            P("frames", "tensor", None),
            P("tensor", None),
            P("tensor", None),
            P("tensor", None, "frames"),
        ),
        out_specs=P("tensor", ("groups", "frames"), None),
        check_vma=False,
    )
```

time: 221 us -> 128 us (0.58)
  waiting for transfers between devices: 185 us -> 0 us
  Pallas kernels: 0 us -> 124 us
  between operations: 13.2 us -> 0.04 us
  matrix products: 12 us -> 0 us
  other arithmetic: 7.81 us -> 0.09 us
  local copies, waits for them, and re-layouts: 1.71 us -> 4.34 us
    pallas_call x0 -> x1, Pallas kernels: none -> 124 us  [local(): pl.pallas_call(functools.partial(kernel, ng, nt, nf, nlo, subs), out_shap...]
    all_gather x3 -> x0, waiting for transfers between devices: 124 us -> none  [the longest x1 64.8 us: local(): every_patch = lax.all_gather(normed, 'tensor', axis=0, tiled=True)]
    reduce_scatter x1 -> x0, waiting for transfers between devices: 60.4 us -> none  [local(): lax.psum_scatter(jnp.einsum('vto,ox->vtx', blended_rows, combined_output,...]
    dot_general x4 -> x0, matrix products: 12 us -> none  [the longest x1 5.89 us: local(): jnp.einsum('qye,ea->qya', every_patch, lax.all_gather(in_local, 'frames',...]
    reduce_sum x4 -> x0, other arithmetic: 3.51 us -> none  [the longest x2 1.9 us: layer_norm(): variance = jnp.mean(centered * centered, axis=-1, keepdims=True)]
    unnamed x8 -> x11, local copies, waits for them, and re-layouts: 0.02 us -> 2.65 us
    convert_element_type x2 -> x1, other arithmetic: 2.56 us -> 0.09 us  [local(): return jnp.transpose(summed, (1, 0, 2)).astype(jnp.bfloat16)]
  transfers between devices with their start and end apart: 4 -> 0, of which waited for: 4 -> 0; matrix products, arithmetic and copies ran while one was open for 4% -> 0% of each run, Pallas kernels for 0% -> 0%
where the time goes in v1:
time: 128 us
  Pallas kernels  124 us (97%)
  local copies, waits for them, and re-layouts  4.34 us (3%)
    pallas_call x1, Pallas kernels, local(): pl.pallas_call(functools.partial(kernel, ng, nt, nf, nlo, subs), out_shap...  124 us
    unnamed x11, local copies, waits for them, and re-layouts  2.65 us

profile of v1, /device:TPU:0, one launch (start us, length us, event | category | flops | bytes accessed | tf_op | source)
XLA Modules:
  0.0 128.2 jit_solution(7877479849221748328)
XLA Ops:
  0.0 0.0 copy-start.4
  0.0 0.0 copy-start.3
  0.0 0.0 copy-start
  0.0 0.0 copy-start.2
  0.0 1.4 %copy.10 = bf16[64,2,3072]{2,0,1:T(8,128)(2,1)S(1)} copy(bf16[64,2,3072]{2,1,0:T(2,128)(2,1)} %param.6) | data formatting | bytes 1572864 | tf_op args[0]
  1.4 0.0 copy-done.4
  1.4 0.0 copy-done.3
  1.4 0.1 copy-done
  1.5 0.0 copy-done.2
  1.5 0.0 copy-start.1
  1.5 1.1 copy-done.1
  2.7 123.7 %shard_map.64 = f32[2,64,3072]{2,1,0:T(8,128)S(1)} custom-call(bf16[2,64,3072]{2,1,0:T(8,128)(2,1)S(1)} %bitcast.8, f32[1,3072]{1,0:T(1,128)S(1)} %bitcast.11, bf16[768,768]{1,0:T(8,128)(2,1)S(1)} %bitcast.9, f32[1,128]{1,0:T(1,128)S(1)} %copy-done.3, f32[1,128]{1,0:T(1,128)S(1)} %copy-done.4, bf16[512,768]{1,0:T(8,128)(2,1)S(1)} %bitcast.10), custom_call_target="tpu_custom_call" | custom-call | tf_op jit(solution)/shard_map/pallas_call | solution.py:309
  126.4 0.1 convert_bitcast_fusion
  126.5 1.7 %copy.8 = bf16[64,2,3072]{2,1,0:T(2,128)(2,1)} copy(bf16[64,2,3072]{2,0,1:T(8,128)(2,1)S(1)} %convert_bitcast_fusion) | data formatting | bytes 1572864 | tf_op jit(solution)/shard_map/convert_element_type | solution.py:341
Async XLA Ops:
  0.0 1.4 %copy-start.4 = (f32[1,128]{1,0:T(1,128)S(1)}, f32[1,128]{1,0:T(1,128)}, u32[]{:S(2)}) copy-start(f32[1,128]{1,0:T(1,128)} %kg_ref.1) | copy-start | bytes 1540
  0.0 1.4 %copy-start.3 = (f32[1,128]{1,0:T(1,128)S(1)}, f32[1,128]{1,0:T(1,128)}, u32[]{:S(2)}) copy-start(f32[1,128]{1,0:T(1,128)} %qg_ref.1) | copy-start | bytes 1540
  0.0 1.5 %copy-start = (bf16[768,1,768]{2,0,1:T(8,128)(2,1)S(1)}, bf16[768,1,768]{2,0,1:T(8,128)(2,1)}, u32[]{:S(2)}) copy-start(bf16[768,1,768]{2,0,1:T(8,128)(2,1)} %param.8) | copy-start | bytes 3538948
  0.0 1.5 %copy-start.2 = (f32[3072]{0:T(1024)S(1)}, f32[3072]{0:T(1024)}, u32[]{:S(2)}) copy-start(f32[3072]{0:T(1024)} %param.7) | copy-start | bytes 36868
  1.5 1.1 copy-start.1

commit v2 on v1

--- a/solution.py
+++ b/solution.py
@@ -19,7 +19,7 @@
 
 
 def kernel(ng, nt, nf, nlo, subs, x_ref, gain_ref, win_ref, qg_ref, kg_ref, wout_ref, out_ref,
-           xg, w_in, w_out, joined, blended, part, rbuf,
+           xg, w_in, w_out, joined, qkv, blended, part, rbuf,
            ag_send, ag_recv, rs_send, rs_recv, ws_send, ws_recv, own_sem):
     g, t, f = lax.axis_index("groups"), lax.axis_index("tensor"), lax.axis_index("frames")
     frames, rows, width = x_ref.shape
@@ -139,22 +139,21 @@
         pl.when(t + 1 < nt)(lambda: act(ag_copy(fr, t, 0)))
         pl.when(t > 0)(lambda: act(ag_copy(fr, t, 1)))
 
-    def ag_step(fr, s, act, wait):
-        b = t - 1 - s
-
-        @pl.when(b >= 0)
-        def _():
-            if wait:
-                ag_copy(fr, b, 0).wait_recv()
-            pl.when(t + 1 < nt)(lambda: act(ag_copy(fr, b, 0)))
-
-        c = t + 1 + s
-
-        @pl.when(c < nt)
-        def _():
-            if wait:
-                ag_copy(fr, c, 1).wait_recv()
-            pl.when(t > 0)(lambda: act(ag_copy(fr, c, 1)))
+    def ag_tick(k, act, wait):
+        for way, count, can_send in ((0, t, t + 1 < nt), (1, nt - 1 - t, t > 0)):
+            @pl.when(k < frames * count)
+            def _(way=way, count=count, can_send=can_send):
+                fr, i = k // jnp.maximum(count, 1), k % jnp.maximum(count, 1)
+                b = t - 1 - i if way == 0 else t + 1 + i
+                if wait:
+                    ag_copy(fr, b, way).wait_recv()
+
+                @pl.when(can_send)
+                def _():
+                    act(ag_copy(fr, b, way))
+                    pl.when((i == count - 1) & (fr + 1 < frames))(lambda: act(ag_copy(fr + 1, t, way)))
+
+            pl.when((k + 1 < frames) & (count == 0) & can_send)(lambda way=way: act(ag_copy(k + 1, t, way)))
 
     def rs_copy(fr, d, way, first):
         slot = d if way == 0 else jnp.where(d == t - 1, nt, d)
@@ -177,28 +176,25 @@
             device_id_type=MESH,
         ).wait_recv()
 
-    def rs_send_on(fr, d, way, edge):
-        @pl.when(edge)
-        def _():
-            rs_copy(fr, d, way, True).start()
-
-        @pl.when(jnp.logical_not(edge))
-        def _():
-            rs_arrived(fr, d)
-            mine = block(part, fr, d)[...].astype(jnp.float32)
-            rbuf[fr, d] = (rbuf[fr, d].astype(jnp.float32) + mine).astype(jnp.bfloat16)
-            rs_copy(fr, d, way, False).start()
+    def rs_edge(fr):
+        for way, here, order in ((0, t == 0, range(nt - 1, 0, -1)), (1, t == nt - 1, range(nt - 1))):
+            @pl.when(here)
+            def _(way=way, order=order):
+                for d in order:
+                    rs_copy(fr, d, way, True).start()
 
     def rs_step(fr, s):
-        d = nt - 1 - s
-        pl.when(d > t)(lambda: rs_send_on(fr, d, 0, t == 0))
-        pl.when(s < t)(lambda: rs_send_on(fr, s, 1, t == nt - 1))
+        for way, d, here in ((0, nt - 1 - s, (nt - 1 - s > t) & (t > 0)), (1, s, (s < t) & (t < nt - 1))):
+            @pl.when(here)
+            def _(way=way, d=d):
+                rs_arrived(fr, d)
+                mine = block(part, fr, d)[...].astype(jnp.float32)
+                rbuf[fr, d] = (rbuf[fr, d].astype(jnp.float32) + mine).astype(jnp.bfloat16)
+                rs_copy(fr, d, way, False).start()
 
     def rs_sent(fr):
         for d in range(nt):
-            @pl.when(d != t)
-            def _():
-                rs_copy(fr, d, 0, True).wait_send()
+            pl.when(d != t)(lambda d=d: rs_copy(fr, d, 0, True).wait_send())
 
     def rs_finish(fr):
         out_ref[fr] = (x_ref[fr].astype(jnp.float32) + block(part, fr, t)[...].astype(jnp.float32)).astype(jnp.float32)
@@ -217,20 +213,26 @@
         values = norm(x_ref[fr].astype(jnp.float32), gain_ref[...]).astype(jnp.bfloat16)
         block(xg, fr, t)[...] = values
 
-    def project(fr):
+    def project(fr, b):
+        at = pl.ds(pl.multiple_of(b * rows, rows), rows)
         tile = 256 if joined.shape[1] % 256 == 0 else joined.shape[1]
-
-        @pl.loop(0, joined.shape[1] // tile)
-        def _(n):
-            cols = pl.ds(pl.multiple_of(n * tile, tile), tile)
+        for n in range(joined.shape[1] // tile):
+            cols = pl.ds(n * tile, tile)
             weight = w_in[:, :, cols].reshape(width, tile)
-            joined[:, cols] = jnp.dot(xg[fr], weight, preferred_element_type=jnp.float32)
-
-        query = norm(joined[:, :head_dim], qg_ref[...]).astype(jnp.bfloat16)
-        key = norm(joined[:, head_dim:2 * head_dim], kg_ref[...]).astype(jnp.bfloat16)
-        value = joined[:, 2 * head_dim:3 * head_dim].astype(jnp.bfloat16)
+            joined[:, cols] = jnp.dot(xg[fr, at, :], weight, preferred_element_type=jnp.float32)
+        bf16 = jnp.bfloat16
+        qkv[at, :head_dim] = norm(joined[:, :head_dim], qg_ref[...]).astype(bf16)
+        qkv[at, head_dim:2 * head_dim] = norm(joined[:, head_dim:2 * head_dim], kg_ref[...]).astype(bf16)
+        qkv[at, 2 * head_dim:] = joined[:, 2 * head_dim:3 * head_dim].astype(bf16)
         raw = joined[:, 3 * head_dim:]
-        blended[:, head_dim:] = (0.5 * raw * (1.0 + lax.erf(raw * math.sqrt(0.5)))).astype(jnp.bfloat16)
+        blended[at, head_dim:] = (0.5 * raw * (1.0 + lax.erf(raw * math.sqrt(0.5)))).astype(bf16)
+
+    def project_step(fr, s):
+        pl.when(t - 1 - s >= 0)(lambda: project(fr, t - 1 - s))
+        pl.when(t + 1 + s < nt)(lambda: project(fr, t + 1 + s))
+
+    def attend():
+        query, key, value = (qkv[:, i * head_dim:(i + 1) * head_dim] for i in range(3))
         scores = lax.dot_general(query, key, (((1,), (1,)), ((), ())), preferred_element_type=jnp.float32)
         exp_scores = jnp.exp(scores * (1.0 / math.sqrt(head_dim)))
         total = jnp.sum(exp_scores, axis=-1, keepdims=True)
@@ -249,48 +251,63 @@
     for w in range(2):
         pltpu.make_async_copy(given[w], held[w].at[f], own_sem.at[w]).start()
     w_own_across(0, start)
-    w_own_sibling(0, start)
     normalise(0)
     ag_own(0, start)
+    w_own_sibling(0, start)
+    w_own_across(1, start)
     for fr in range(1, frames):
         normalise(fr)
-
-    tasks = [functools.partial(w_relay, 0, sub, start, True) for sub in range(subs)]
-    tasks += [functools.partial(w_own_across, 1, start), functools.partial(w_own_sibling, 1, start)]
-    tasks += [functools.partial(w_relay_two, 0, sub, start, True) for sub in range(subs)]
-    tasks += [functools.partial(w_relay, 1, sub, start, True) for sub in range(subs)]
-    done = 0
-    for s in range(nt - 1):
-        until = -(-len(tasks) * (s + 1) // (nt - 1))
-        for task in tasks[done:until]:
+    w_own_sibling(1, start)
+
+    def relays(step, w, lowest, highest):
+        return [functools.partial(step, w, sub, start, True) for sub in range(lowest, min(highest, subs))]
+
+    groups = [
+        relays(w_relay, 0, 0, 1),
+        relays(w_relay, 0, 1, subs) + relays(w_relay_two, 0, 0, 1) + relays(w_relay, 1, 0, 1),
+        relays(w_relay_two, 0, 1, subs) + relays(w_relay, 1, 1, subs) + relays(w_relay_two, 1, 0, subs - 1),
+    ]
+    for k in range(nt - 2):
+        for task in groups.pop(0) if groups else ():
             task()
-        done = until
-        ag_step(0, s, start, True)
+        ag_tick(k, start, True)
+    for task in sum(groups, []):
+        task()
+    w_finish(0)
+    project(0, t)
+    pl.loop(0, nt - 2)(lambda s: project_step(0, s))
+    ag_tick(nt - 2, start, True)
+    project_step(0, nt - 2)
+    for task in relays(w_relay_two, 1, subs - 1, subs):
+        task()
+    attend()
+    w_finish(1)
     for fr in range(frames):
+        contribute(fr)
+        rs_edge(fr)
         if fr + 1 < frames:
-            ag_own(fr + 1, start)
-        if fr == 0:
-            w_finish(0)
-        project(fr)
-        if fr == 0:
-            for sub in range(subs):
-                w_relay_two(1, sub, start, True)
-            w_finish(1)
-        contribute(fr)
-        for s in range(nt - 1):
+            project(fr + 1, t)
+
+        @pl.loop(0, nt - 1)
+        def _(s, fr=fr):
             if fr + 1 < frames:
-                ag_step(fr + 1, s, start, True)
+                ag_tick((fr + 1) * (nt - 1) + s, start, True)
             rs_step(fr, s)
+            if fr + 1 < frames:
+                project_step(fr + 1, s)
+
+        if fr + 1 < frames:
+            attend()
     for fr in range(frames):
         rs_finish(fr)
 
     for w in range(2):
         w_sent(w)
     for fr in range(frames):
-        ag_own(fr, sent)
-        for s in range(nt - 1):
-            ag_step(fr, s, sent, False)
         rs_sent(fr)
+    ag_own(0, sent)
+    for k in range(frames * (nt - 1)):
+        ag_tick(k, sent, False)
 
 
 def local(ng, nt, nf, patches, ln_gain, in_weight, q_gain, k_gain, out_weight):
@@ -315,7 +332,8 @@
             pltpu.VMEM((frames, everyone, width), bf16),
             pltpu.VMEM((nf, depth, joined_cols), bf16),
             pltpu.VMEM((nf, out_rows, out_cols), bf16),
-            pltpu.VMEM((everyone, joined_cols), f32),
+            pltpu.VMEM((rows, joined_cols), f32),
+            pltpu.VMEM((everyone, 3 * q_gain.shape[1]), bf16),
             pltpu.VMEM((everyone, out_rows), bf16),
             pltpu.VMEM((frames, everyone, width), bf16),
             pltpu.VMEM((frames, nt + 1, rows, width), bf16),

time: 128 us -> 117 us (0.914)
  Pallas kernels: 124 us -> 112 us
    pallas_call x1, Pallas kernels: 124 us -> 112 us  [local(): pl.pallas_call(functools.partial(kernel, ng, nt, nf, nlo, subs), out_shap...]
where the time goes in v2:
time: 117 us
  Pallas kernels  112 us (96%)
  local copies, waits for them, and re-layouts  4.34 us (4%)
    pallas_call x1, Pallas kernels, local(): pl.pallas_call(functools.partial(kernel, ng, nt, nf, nlo, subs), out_shap...  112 us
    unnamed x11, local copies, waits for them, and re-layouts  2.65 us

profile of v2, /device:TPU:0, one launch (start us, length us, event | category | flops | bytes accessed | tf_op | source)
XLA Modules:
  0.0 116.9 jit_solution(18431945563050494393)
XLA Ops:
  0.0 0.0 copy-start.4
  0.0 0.0 copy-start.3
  0.0 0.0 copy-start
  0.0 0.0 copy-start.2
  0.0 1.4 %copy.10 = bf16[64,2,3072]{2,0,1:T(8,128)(2,1)S(1)} copy(bf16[64,2,3072]{2,1,0:T(2,128)(2,1)} %param.6) | data formatting | bytes 1572864 | tf_op args[0]
  1.4 0.0 copy-done.4
  1.4 0.0 copy-done.3
  1.4 0.1 copy-done
  1.5 0.0 copy-done.2
  1.5 0.0 copy-start.1
  1.5 1.1 copy-done.1
  2.7 112.5 %shard_map.64 = f32[2,64,3072]{2,1,0:T(8,128)S(1)} custom-call(bf16[2,64,3072]{2,1,0:T(8,128)(2,1)S(1)} %bitcast.8, f32[1,3072]{1,0:T(1,128)S(1)} %bitcast.11, bf16[768,768]{1,0:T(8,128)(2,1)S(1)} %bitcast.9, f32[1,128]{1,0:T(1,128)S(1)} %copy-done.3, f32[1,128]{1,0:T(1,128)S(1)} %copy-done.4, bf16[512,768]{1,0:T(8,128)(2,1)S(1)} %bitcast.10), custom_call_target="tpu_custom_call" | custom-call | tf_op jit(solution)/shard_map/pallas_call | solution.py:326
  115.2 0.1 convert_bitcast_fusion
  115.3 1.7 %copy.8 = bf16[64,2,3072]{2,1,0:T(2,128)(2,1)} copy(bf16[64,2,3072]{2,0,1:T(8,128)(2,1)S(1)} %convert_bitcast_fusion) | data formatting | bytes 1572864 | tf_op jit(solution)/shard_map/convert_element_type | solution.py:359
Async XLA Ops:
  0.0 1.4 %copy-start.4 = (f32[1,128]{1,0:T(1,128)S(1)}, f32[1,128]{1,0:T(1,128)}, u32[]{:S(2)}) copy-start(f32[1,128]{1,0:T(1,128)} %kg_ref.1) | copy-start | bytes 1540
  0.0 1.4 %copy-start.3 = (f32[1,128]{1,0:T(1,128)S(1)}, f32[1,128]{1,0:T(1,128)}, u32[]{:S(2)}) copy-start(f32[1,128]{1,0:T(1,128)} %qg_ref.1) | copy-start | bytes 1540
  0.0 1.5 %copy-start = (bf16[768,1,768]{2,0,1:T(8,128)(2,1)S(1)}, bf16[768,1,768]{2,0,1:T(8,128)(2,1)}, u32[]{:S(2)}) copy-start(bf16[768,1,768]{2,0,1:T(8,128)(2,1)} %param.8) | copy-start | bytes 3538948
  0.0 1.5 %copy-start.2 = (f32[3072]{0:T(1024)S(1)}, f32[3072]{0:T(1024)}, u32[]{:S(2)}) copy-start(f32[3072]{0:T(1024)} %param.7) | copy-start | bytes 36868
  1.5 1.1 copy-start.1

commit v3 on v2

--- a/solution.py
+++ b/solution.py
@@ -100,14 +100,14 @@
                 if nlo > 1:
                     act(move(w, shard, section, sub, last, sibling))
 
-    def w_finish(w):
+    def w_ready(w, j):
+        pair = lax.rem(hi + j, nhi)
         if nlo > 1:
-            for j in range(nhi):
-                shard = j * nlo + (nlo - 1 - lo)
-                for section in range(ng):
-                    for sub in range(subs):
-                        move(w, shard, section, sub, 0, sibling).wait_recv()
-        pltpu.make_async_copy(given[w], held[w].at[f], own_sem.at[w]).wait()
+            for section in range(ng):
+                for sub in range(subs):
+                    move(w, pair * nlo + (nlo - 1 - lo), section, sub, 0, sibling).wait_recv()
+        if j == 0:
+            pltpu.make_async_copy(given[w], held[w].at[f], own_sem.at[w]).wait()
 
     def start(copy):
         copy.start()
@@ -155,59 +155,64 @@
 
             pl.when((k + 1 < frames) & (count == 0) & can_send)(lambda way=way: act(ag_copy(k + 1, t, way)))
 
-    def rs_copy(fr, d, way, first):
+    def sums(fr, c, d):
+        return part.at[fr, c, pl.ds(pl.multiple_of(d * rows, rows), rows), :]
+
+    def rs_copy(fr, c, d, way, first):
         slot = d if way == 0 else jnp.where(d == t - 1, nt, d)
         return pltpu.make_async_remote_copy(
-            src_ref=block(part, fr, d) if first else rbuf.at[fr, d],
-            dst_ref=rbuf.at[fr, slot],
-            send_sem=rs_send.at[fr, d],
-            recv_sem=rs_recv.at[fr, slot],
+            src_ref=sums(fr, c, d) if first else rbuf.at[fr, c, d],
+            dst_ref=rbuf.at[fr, c, slot],
+            send_sem=rs_send.at[fr, c, d],
+            recv_sem=rs_recv.at[fr, c, slot],
             device_id=right if way == 0 else left,
             device_id_type=MESH,
         )
 
-    def rs_arrived(fr, slot):
+    def rs_arrived(fr, c, slot):
         pltpu.make_async_remote_copy(
-            src_ref=rbuf.at[fr, slot],
-            dst_ref=rbuf.at[fr, slot],
-            send_sem=rs_send.at[fr, 0],
-            recv_sem=rs_recv.at[fr, slot],
+            src_ref=rbuf.at[fr, c, slot],
+            dst_ref=rbuf.at[fr, c, slot],
+            send_sem=rs_send.at[fr, c, 0],
+            recv_sem=rs_recv.at[fr, c, slot],
             device_id=right,
             device_id_type=MESH,
         ).wait_recv()
 
-    def rs_edge(fr):
+    def rs_edge(fr, c):
         for way, here, order in ((0, t == 0, range(nt - 1, 0, -1)), (1, t == nt - 1, range(nt - 1))):
             @pl.when(here)
             def _(way=way, order=order):
                 for d in order:
-                    rs_copy(fr, d, way, True).start()
-
-    def rs_step(fr, s):
+                    rs_copy(fr, c, d, way, True).start()
+
+    def rs_step(fr, c, s):
         for way, d, here in ((0, nt - 1 - s, (nt - 1 - s > t) & (t > 0)), (1, s, (s < t) & (t < nt - 1))):
             @pl.when(here)
             def _(way=way, d=d):
-                rs_arrived(fr, d)
-                mine = block(part, fr, d)[...].astype(jnp.float32)
-                rbuf[fr, d] = (rbuf[fr, d].astype(jnp.float32) + mine).astype(jnp.bfloat16)
-                rs_copy(fr, d, way, False).start()
-
-    def rs_sent(fr):
+                rs_arrived(fr, c, d)
+                mine = sums(fr, c, d)[...].astype(jnp.float32)
+                rbuf[fr, c, d] = (rbuf[fr, c, d].astype(jnp.float32) + mine).astype(jnp.bfloat16)
+                rs_copy(fr, c, d, way, False).start()
+
+    def rs_sent(fr, c):
         for d in range(nt):
-            pl.when(d != t)(lambda d=d: rs_copy(fr, d, 0, True).wait_send())
-
-    def rs_finish(fr):
-        out_ref[fr] = (x_ref[fr].astype(jnp.float32) + block(part, fr, t)[...].astype(jnp.float32)).astype(jnp.float32)
+            pl.when(d != t)(lambda d=d: rs_copy(fr, c, d, 0, True).wait_send())
+
+    def rs_finish(fr, c):
+        size = width // nhi
+        cols = pl.ds(pl.multiple_of(c * size, size), size)
+        out_ref[fr, :, cols] = x_ref[fr, :, cols].astype(jnp.float32) + sums(fr, c, t)[...].astype(jnp.float32)
 
         @pl.when(t > 0)
         def _():
-            rs_arrived(fr, t)
-            out_ref[fr] += rbuf[fr, t].astype(jnp.float32)
+            rs_arrived(fr, c, t)
+            out_ref[fr, :, cols] += rbuf[fr, c, t].astype(jnp.float32)
 
         @pl.when(t + 1 < nt)
         def _():
-            rs_arrived(fr, nt)
-            out_ref[fr] += rbuf[fr, nt].astype(jnp.float32)
+            rs_arrived(fr, c, nt)
+            out_ref[fr, :, cols] += rbuf[fr, c, nt].astype(jnp.float32)
 
     def normalise(fr):
         values = norm(x_ref[fr].astype(jnp.float32), gain_ref[...]).astype(jnp.bfloat16)
@@ -239,13 +244,11 @@
         attended = jnp.dot(exp_scores.astype(jnp.bfloat16), value, preferred_element_type=jnp.float32)
         blended[:, :head_dim] = (attended / total).astype(jnp.bfloat16)
 
-    def contribute(fr):
+    def contribute(fr, c):
         cols = w_out.shape[2]
-
-        @pl.loop(0, nf)
-        def _(n):
-            part[fr, :, pl.ds(pl.multiple_of(n * cols, cols), cols)] = jnp.dot(
-                blended[...], w_out[n], preferred_element_type=jnp.float32
+        for n in range(nlo):
+            part[fr, c, :, n * cols:(n + 1) * cols] = jnp.dot(
+                blended[...], w_out[c * nlo + n], preferred_element_type=jnp.float32
             ).astype(jnp.bfloat16)
 
     for w in range(2):
@@ -273,38 +276,49 @@
         ag_tick(k, start, True)
     for task in sum(groups, []):
         task()
-    w_finish(0)
+    for j in range(nhi):
+        w_ready(0, j)
     project(0, t)
     pl.loop(0, nt - 2)(lambda s: project_step(0, s))
     ag_tick(nt - 2, start, True)
     project_step(0, nt - 2)
-    for task in relays(w_relay_two, 1, subs - 1, subs):
-        task()
     attend()
-    w_finish(1)
+    chunks = [lax.rem(hi + j, nhi) for j in range(nhi)]
     for fr in range(frames):
-        contribute(fr)
-        rs_edge(fr)
+        for j, c in enumerate(chunks):
+            if fr == 0:
+                if j == min(1, nhi - 1):
+                    for task in relays(w_relay_two, 1, subs - 1, subs):
+                        task()
+                w_ready(1, j)
+            contribute(fr, c)
+            rs_edge(fr, c)
         if fr + 1 < frames:
             project(fr + 1, t)
+        if fr > 0:
+            for c in chunks:
+                rs_finish(fr - 1, c)
 
         @pl.loop(0, nt - 1)
         def _(s, fr=fr):
             if fr + 1 < frames:
                 ag_tick((fr + 1) * (nt - 1) + s, start, True)
-            rs_step(fr, s)
+            for i in range(nhi):
+                m = s * nhi + i
+                rs_step(fr, lax.rem(hi + m // (nt - 1), nhi), m % (nt - 1))
             if fr + 1 < frames:
                 project_step(fr + 1, s)
 
         if fr + 1 < frames:
             attend()
-    for fr in range(frames):
-        rs_finish(fr)
+    for c in chunks:
+        rs_finish(frames - 1, c)
 
     for w in range(2):
         w_sent(w)
     for fr in range(frames):
-        rs_sent(fr)
+        for c in range(nhi):
+            rs_sent(fr, c)
     ag_own(0, sent)
     for k in range(frames * (nt - 1)):
         ag_tick(k, sent, False)
@@ -335,12 +349,12 @@
             pltpu.VMEM((rows, joined_cols), f32),
             pltpu.VMEM((everyone, 3 * q_gain.shape[1]), bf16),
             pltpu.VMEM((everyone, out_rows), bf16),
-            pltpu.VMEM((frames, everyone, width), bf16),
-            pltpu.VMEM((frames, nt + 1, rows, width), bf16),
+            pltpu.VMEM((frames, nhi, everyone, width // nhi), bf16),
+            pltpu.VMEM((frames, nhi, nt + 1, rows, width // nhi), bf16),
             dma((frames, 2, nt)),
             dma((frames, nt)),
-            dma((frames, nt)),
-            dma((frames, nt + 1)),
+            dma((frames, nhi, nt)),
+            dma((frames, nhi, nt + 1)),
             dma((2, nf, ng, subs, slots)),
             dma((2, nf, ng, subs)),
             dma((2,)),

time: 117 us -> 104 us (0.89)
  Pallas kernels: 112 us -> 99.3 us
    pallas_call x1, Pallas kernels: 112 us -> 99.3 us  [local(): pl.pallas_call(functools.partial(kernel, ng, nt, nf, nlo, subs), out_shap...]
where the time goes in v3:
time: 104 us
  Pallas kernels  99.3 us (95%)
  local copies, waits for them, and re-layouts  4.34 us (4%)
    pallas_call x1, Pallas kernels, local(): pl.pallas_call(functools.partial(kernel, ng, nt, nf, nlo, subs), out_shap...  99.3 us
    unnamed x11, local copies, waits for them, and re-layouts  2.65 us

profile of v3, /device:TPU:0, one launch (start us, length us, event | category | flops | bytes accessed | tf_op | source)
XLA Modules:
  0.0 103.7 jit_solution(3623240230794240755)
XLA Ops:
  0.0 0.0 copy-start.4
  0.0 0.0 copy-start.3
  0.0 0.0 copy-start
  0.0 0.0 copy-start.2
  0.0 1.4 %copy.10 = bf16[64,2,3072]{2,0,1:T(8,128)(2,1)S(1)} copy(bf16[64,2,3072]{2,1,0:T(2,128)(2,1)} %param.6) | data formatting | bytes 1572864 | tf_op args[0]
  1.4 0.0 copy-done.4
  1.4 0.0 copy-done.3
  1.4 0.1 copy-done
  1.5 0.0 copy-done.2
  1.5 0.0 copy-start.1
  1.5 1.1 %copy-done.1 = bf16[1,512,768]{2,1,0:T(8,128)(2,1)S(1)} copy-done((bf16[1,512,768]{2,1,0:T(8,128)(2,1)S(1)}, bf16[1,512,768]{2,1,0:T(8,128)(2,1)}, u32[]{:S(2)}) %copy-start.1) | copy-done | bytes 786456
  2.7 99.3 %shard_map.64 = f32[2,64,3072]{2,1,0:T(8,128)S(1)} custom-call(bf16[2,64,3072]{2,1,0:T(8,128)(2,1)S(1)} %bitcast.8, f32[1,3072]{1,0:T(1,128)S(1)} %bitcast.11, bf16[768,768]{1,0:T(8,128)(2,1)S(1)} %bitcast.9, f32[1,128]{1,0:T(1,128)S(1)} %copy-done.3, f32[1,128]{1,0:T(1,128)S(1)} %copy-done.4, bf16[512,768]{1,0:T(8,128)(2,1)S(1)} %bitcast.10), custom_call_target="tpu_custom_call" | custom-call | tf_op jit(solution)/shard_map/pallas_call | solution.py:340
  102.0 0.1 convert_bitcast_fusion
  102.1 1.7 %copy.8 = bf16[64,2,3072]{2,1,0:T(2,128)(2,1)} copy(bf16[64,2,3072]{2,0,1:T(8,128)(2,1)S(1)} %convert_bitcast_fusion) | data formatting | bytes 1572864 | tf_op jit(solution)/shard_map/convert_element_type | solution.py:373
Async XLA Ops:
  0.0 1.4 %copy-start.4 = (f32[1,128]{1,0:T(1,128)S(1)}, f32[1,128]{1,0:T(1,128)}, u32[]{:S(2)}) copy-start(f32[1,128]{1,0:T(1,128)} %kg_ref.1) | copy-start | bytes 1540
  0.0 1.4 %copy-start.3 = (f32[1,128]{1,0:T(1,128)S(1)}, f32[1,128]{1,0:T(1,128)}, u32[]{:S(2)}) copy-start(f32[1,128]{1,0:T(1,128)} %qg_ref.1) | copy-start | bytes 1540
  0.0 1.5 %copy-start = (bf16[768,1,768]{2,0,1:T(8,128)(2,1)S(1)}, bf16[768,1,768]{2,0,1:T(8,128)(2,1)}, u32[]{:S(2)}) copy-start(bf16[768,1,768]{2,0,1:T(8,128)(2,1)} %param.8) | copy-start | bytes 3538948
  0.0 1.5 %copy-start.2 = (f32[3072]{0:T(1024)S(1)}, f32[3072]{0:T(1024)}, u32[]{:S(2)}) copy-start(f32[3072]{0:T(1024)} %param.7) | copy-start | bytes 36868
  1.5 1.1 %copy-start.1 = (bf16[1,512,768]{2,1,0:T(8,128)(2,1)S(1)}, bf16[1,512,768]{2,1,0:T(8,128)(2,1)}, u32[]{:S(2)}) copy-start(bf16[1,512,768]{2,1,0:T(8,128)(2,1)} %param.11) | copy-start | bytes 2359300
